TPU v7x, 32 devices: a whole 2x2x4 slice. The times are simulated.
32 devices in a mesh: horiz: 8 (over z, y), lev: 4 (over x, core).
Axes of the slice: x: 2, y: 2, z: 4, core: 2. Of those that a mesh axis runs over, the one named last changes fastest.
Arguments:
- control: float32 [64, 32, 4096], P('lev', None, 'horiz'), may hold values from -6 to 6
- members: bfloat16 [64, 4, 32, 4096], P('lev', None, None, 'horiz'), may hold values from -6 to 6
- extinction: float32 [4], replicated, may hold values from 0.5 to 2
- kernels: bfloat16 [4096, 64, 128], P('horiz', 'lev'), may hold values from 0 to 1
- innovation: bfloat16 [4096, 128], P('horiz'), may hold values from -16 to 16
- obs_weight: bfloat16 [4096, 128], P('horiz'), may hold values from 0.25 to 4
- owners: int32 [4096, 1], P('horiz'), may hold values from 0 to 7; in each aligned block of 512 rows (0 to 511, 512 to 1023, ...) at most 128 rows name the same one
- pixel_columns: int32 [4096, 128], P('horiz'), may hold values from 0 to 511
- pixel_counts: int32 [4096], P('horiz'), may hold values from 1 to 128
Outputs:
- gradient: float32 [64, 32, 4096], P('lev', None, 'horiz')
Inputs may be any that keep to these rules, and one draw needn't show every extreme that they name: `owners`: among the 512 blocks of one index of horiz, no owner is named more than 128 times, and in some index's blocks one owner is named exactly 128 times.
All inputs are finite; a program needn't handle non-finite values.
Results may differ from a plain program's by a relative error of at most 0.0037.
Values may be sent and summed in bfloat16 or wider, within the bound.
A program may use at most 128 MiB of HBM per device.

v0:
```python
import math
import jax
import jax.numpy as jnp
from jax import lax
from jax.sharding import PartitionSpec as P

LEV = 64
HALF = 4


def with_halo(value, sides, width):
    for axis, dim in sides:
        devices, length = (lax.axis_size(axis), value.shape[dim])
        up = [(i, (i + 1) % devices) for i in range(devices - 1)]
        down = [(j, i) for i, j in up]
        last = lax.slice_in_dim(value, length - width, length, axis=dim)
        first = lax.slice_in_dim(value, 0, width, axis=dim)
        before = lax.ppermute(last, axis, up)
        after = lax.ppermute(first, axis, down)
        value = jnp.concatenate([before, value, after], axis=dim)
    return value


def level_matrix():
    index_levels = jnp.arange(LEV, dtype=jnp.float32)
    spread = LEV / 8.0
    distance = index_levels[:, None] - index_levels[None, :]
    matrix = jnp.exp(-distance * distance / (2.0 * spread * spread)) / (2.5066283 * spread)
    return matrix.astype(jnp.bfloat16)


def column_taps():
    offsets = jnp.arange(2 * HALF + 1, dtype=jnp.float32) - HALF
    spread = HALF / 2.0
    weights = jnp.exp(-offsets * offsets / (2.0 * spread * spread))
    return weights / jnp.sum(weights)


def smooth_columns(values):
    tap_weights = column_taps()
    span = values.shape[2]
    padded = with_halo(values, (("horiz", 2),), HALF)
    running = jnp.zeros(values.shape, jnp.float32)
    for offset in range(2 * HALF + 1):
        running = running + tap_weights[offset] * padded[:, :, offset : offset + span]
    return running


def evolve_pixels(kernel_rows, picked):
    return jnp.sum(kernel_rows.astype(jnp.float32) * picked, axis=1)


def pixel_misfit(evolved, innov_rows, weight_rows, count_rows):
    pixel_width = evolved.shape[1]
    live_pixels = jnp.arange(pixel_width, dtype=jnp.int32)[None, :] < count_rows[:, None]
    return jnp.where(
        live_pixels,
        weight_rows.astype(jnp.float32) * (evolved - innov_rows.astype(jnp.float32)),
        0.0,
    )


def column_onehot(column_block, col_count):
    return (
        jnp.arange(col_count, dtype=jnp.int32)[:, None, None] == column_block[None, :, :]
    ).astype(jnp.float32)


def body(
    control,
    members,
    extinction,
    kernels,
    innovation,
    obs_weight,
    owners,
    pixel_columns,
    pixel_counts,
):
    lev_local, mem_count, col_count = control.shape
    level_loc = level_matrix()
    first_level = lax.axis_index("lev") * lev_local
    mine_rows = lax.dynamic_slice_in_dim(level_loc, first_level, lev_local, 0)
    mine_cols = lax.dynamic_slice_in_dim(level_loc, first_level, lev_local, 1)
    scale = 1.0 / math.sqrt(mem_count)
    control_b = control.astype(jnp.bfloat16)
    section = mine_rows
    vertical = jnp.einsum(
        "ab,bmc->amc",
        section,
        lax.all_gather(control_b, "lev", axis=0, tiled=True),
        preferred_element_type=jnp.float32,
    )
    increment = smooth_columns(vertical)
    mixed = extinction[0] * members[:, 0].astype(jnp.float32)
    for species in range(1, members.shape[1]):
        mixed = mixed + extinction[species] * members[:, species].astype(jnp.float32)
    column_field = jnp.sum(mixed * increment, axis=1) * scale
    owner_ids = owners[:, 0]
    horiz_count = lax.axis_size("horiz")
    blocks_local = owner_ids.shape[0]
    pixel_width = pixel_columns.shape[1]
    capacity = max(2, 2 * (blocks_local // horiz_count))
    total_slots = horiz_count * capacity
    owner_range = jnp.arange(horiz_count, dtype=jnp.int32)
    belongs = (owner_ids[:, None] == owner_range[None, :]).astype(jnp.float32)
    block_range = jnp.arange(blocks_local, dtype=jnp.int32)
    strictly_lower = (block_range[:, None] > block_range[None, :]).astype(jnp.float32)
    earlier = jnp.dot(strictly_lower, belongs, precision=lax.Precision.HIGHEST)
    slot_index = jnp.sum(earlier * belongs, axis=1).astype(jnp.int32)
    target_slot = owner_ids * capacity + slot_index
    placement = jnp.arange(total_slots, dtype=jnp.int32)[:, None] == target_slot[None, :]
    place_half = placement.astype(jnp.bfloat16)
    kernel_buf = (
        jnp.dot(place_half, kernels.reshape(blocks_local, -1), preferred_element_type=jnp.float32)
        .astype(jnp.bfloat16)
        .reshape((total_slots,) + kernels.shape[1:])
    )
    paired = jnp.stack([innovation, obs_weight], 1).reshape(blocks_local, -1)
    value_buf = (
        jnp.dot(place_half, paired, preferred_element_type=jnp.float32)
        .astype(jnp.bfloat16)
        .reshape(total_slots, 2, pixel_width)
    )
    index_rows = jnp.concatenate([pixel_columns, pixel_counts[:, None]], 1).astype(jnp.float32)
    index_buf = jnp.dot(
        placement.astype(jnp.float32), index_rows, precision=lax.Precision.HIGHEST
    ).astype(jnp.int32)
    column_buf = index_buf[:, :pixel_width]
    count_buf = index_buf[:, pixel_width]
    kernel_in, value_in = (
        lax.all_to_all(kernel_buf, "horiz", split_axis=0, concat_axis=0, tiled=True),
        lax.all_to_all(value_buf, "horiz", split_axis=0, concat_axis=0, tiled=True),
    )
    column_in, count_in = (
        lax.all_to_all(column_buf, "horiz", split_axis=0, concat_axis=0, tiled=True),
        lax.all_to_all(count_buf, "horiz", split_axis=0, concat_axis=0, tiled=True),
    )
    slot_group = math.gcd(total_slots, 64)
    group_count = total_slots // slot_group
    kernel_groups = kernel_in.reshape(group_count, slot_group, lev_local, pixel_width)
    column_groups = column_in.reshape(group_count, slot_group, pixel_width)

    def forward_group(operands):
        kernel_block, column_block = operands
        onehot = column_onehot(column_block, col_count)
        picked = jnp.einsum("ac,cgp->gap", column_field, onehot, precision=lax.Precision.HIGHEST)
        return evolve_pixels(kernel_block, picked)

    local_sums = lax.map(forward_group, (kernel_groups, column_groups)).reshape(
        total_slots, pixel_width
    )
    evolved = lax.psum(local_sums, "lev")
    misfit = pixel_misfit(evolved, value_in[:, 0], value_in[:, 1], count_in)
    misfit_groups = misfit.reshape(group_count, slot_group, pixel_width)

    def adjoint_group(running, operands):
        kernel_block, column_block, misfit_block = operands
        onehot = column_onehot(column_block, col_count)
        contrib = kernel_block.astype(jnp.float32) * misfit_block[:, None, :]
        return (
            running + jnp.einsum("gap,cgp->ac", contrib, onehot, precision=lax.Precision.HIGHEST),
            None,
        )

    field_grad, unused = lax.scan(
        adjoint_group,
        jnp.zeros((lev_local, col_count), jnp.float32),
        (kernel_groups, column_groups, misfit_groups),
    )
    member_grad = mixed * field_grad[:, None, :] * scale
    smoothed_b = smooth_columns(member_grad).astype(jnp.bfloat16)
    section = mine_cols
    adjoint_field = jnp.einsum(
        "ba,bmc->amc",
        section,
        lax.all_gather(smoothed_b, "lev", axis=0, tiled=True),
        preferred_element_type=jnp.float32,
    )
    return control + adjoint_field


def solution(mesh):
    placed = (
        P("lev", None, "horiz"),
        P("lev", None, None, "horiz"),
        P(),
        P("horiz", "lev", None),
        P("horiz", None),
        P("horiz", None),
        P("horiz", None),
        P("horiz", None),
        P("horiz"),
    )
    return jax.shard_map(
        body, mesh=mesh, in_specs=placed, out_specs=P("lev", None, "horiz"), check_vma=False
    )
```

profile of v0, /device:TPU:0, one launch (start us, length us, event | category | flops | bytes accessed | tf_op | source)
XLA Modules:
  0.0 520.4 jit_solution(10034451160661777724)
XLA Ops:
  9.2 2.3 fusion.19
  12.4 7.3 %all-to-all-start.3 = ((s32[8,128,128]{1,2,0:T(8,128)}), s32[8,128,128]{1,2,0:T(8,128)S(1)}, u32[]{:S(2)}, u32[]{:S(2)}) async-start(s32[8,128,128]{1,2,0:T(8,128)} %copy_bitcast_fusion), calls=%async_computation.3 | async-start | bytes 1048576 | tf_op jit(solution)/shard_map/all_to_all | solution.py:136
  19.7 2.4 convert_bitcast_fusion
  22.1 3.4 copy.75
  25.5 8.7 %all-to-all-done.3 = s32[8,128,128]{1,2,0:T(8,128)S(1)} async-done(((s32[8,128,128]{1,2,0:T(8,128)}), s32[8,128,128]{1,2,0:T(8,128)S(1)}, u32[]{:S(2)}, u32[]{:S(2)}) %all-to-all-start.3) | async-done | bytes 524320 | tf_op jit(solution)/shard_map/all_to_all | solution.py:136
  35.0 4.7 all-to-all-start
  39.8 1.4 copy.90
  43.6 1.4 slice_bitcast_fusion.1
  45.0 1.4 fusion.18
  46.4 1.4 fusion.91
  47.7 18.3 %all-gather.3.cloned.1.call-done = bf16[64,32,512]{2,0,1:T(8,128)(2,1)} async-done(((bf16[16,32,512]{2,0,1:T(8,128)(2,1)}), bf16[64,32,512]{2,0,1:T(8,128)(2,1)}) %all-gather.3.cloned.1.call-update) | async-done | bytes 2097168 | tf_op jit(solution)/shard_map/all_gather | solution.py:91
  66.1 2.0 fusion.82
  68.8 1.3 collective-permute-start.1
  70.1 5.3 %collective-permute-start = (f32[16,32,4]{2,0,1:T(8,128)S(1)}, f32[16,32,4]{2,0,1:T(8,128)}, u32[]{:S(2)}, u32[]{:S(2)}) collective-permute-start(f32[16,32,4]{2,0,1:T(8,128)S(1)} %get-tuple-element.107), channel_id=1, source_target_pairs={{0,4},{4,8},{8,12},{12,16},{16,20},{20,24},{24,28},{1,5},{5,9},{9,... | collective-permute-start | bytes 24584 | tf_op jit(solution)/shard_map/ppermute | solution.py:18
  78.2 12.2 %collective-permute-done.1 = f32[16,32,4]{2,0,1:T(8,128)} collective-permute-done((f32[16,32,4]{2,0,1:T(8,128)}, f32[16,32,4]{2,0,1:T(8,128)}, u32[]{:S(2)}, u32[]{:S(2)}) %collective-permute-start.1) | collective-permute-done | bytes 8224 | tf_op jit(solution)/shard_map/ppermute | solution.py:19
  90.4 13.0 %fusion.47 = (f32[16,512]{1,0:T(8,128)S(1)}, f32[16,1,32,512]{3,0,2,1:T(8,128)S(1)}) fusion(f32[16,32,512]{2,0,1:T(8,128)S(1)} %fusion.82, f32[16,32,4]{2,0,1:T(8,128)} %collective-permute-done.1, f32[16,32,4]{2,0,1:T(8,128)} %collective-permute-done, f32[]{:T(128)} %bitcast.32, f32[]{:T(128)} %bitcast.31, f32[]{:T(128)} %bitcast.30, f32[]{:T(128)} %bitcast.29, ...), kind=kLoop, calls=%fused_computation.82 | loop fusion | flops 9953280 | bytes 4243508 | tf_op jit(solution)/shard_map/reduce_sum | solution.py:98
  103.5 30.8 %all-to-all-done = bf16[1024,16,128]{2,1,0:T(8,128)(2,1)} async-done(((bf16[1024,16,128]{2,1,0:T(8,128)(2,1)}), bf16[1024,16,128]{2,1,0:T(8,128)(2,1)}, u32[]{:S(2)}, u32[]{:S(2)}) %all-to-all-start) | async-done | bytes 4194336 | tf_op jit(solution)/shard_map/all_to_all | solution.py:132
  134.3 19.4 %all-to-all-start.2 = ((bf16[1024,2,128]{2,1,0:T(2,128)(2,1)}), bf16[1024,2,128]{2,1,0:T(2,128)(2,1)S(1)}, u32[]{:S(2)}, u32[]{:S(2)}) async-start(bf16[1024,2,128]{2,1,0:T(2,128)(2,1)} %copy.58), calls=%async_computation.2 | async-start | bytes 1048576 | tf_op jit(solution)/shard_map/all_to_all | solution.py:133
  154.0 123.3 %while.21 = (s32[]{:T(128)}, f32[16,64,128]{2,1,0:T(8,128)}, bf16[16,64,16,128]{3,2,1,0:T(8,128)(2,1)}, s32[16,64,128]{2,1,0:T(8,128)}, f32[16,512]{1,0:T(8,128)S(1)}, /*index=5*/s32[]{:T(128)}) while((s32[]{:T(128)}, f32[16,64,128]{2,1,0:T(8,128)}, bf16[16,64,16,128]{3,2,1,0:T(8,128)(2,1)}, s32[16,64,128]{2,1,0:T(8,128)}, ...), condition=%wide.region_5.6_spmd, body=%wide.region_3.5_spmd.sunk | while | flops 809885696 | bytes 491609 | solution.py:150
  154.7 6.3 %fusion.104 = f32[64,128]{1,0:T(8,128)S(1)} fusion(s32[64,128]{1,0:T(8,128)S(1)} %dynamic-slice_bitcast_fusion.6, bf16[16,64,16,128]{3,2,1,0:T(8,128)(2,1)} %get-tuple-element.200, s32[]{:T(128)S(6)} %copy.98, f32[16,512]{1,0:T(8,128)S(1)} %get-tuple-element.202), kind=kOutput, calls=%fused_computation.5.clone.1 | convolution fusion | flops 809885696 | bytes 360452 | tf_op jit(solution)/shard_map/while/body/eval_jaxpr/ac,cgp->gap/dot_general | solution.py:147
  162.4 6.3 %fusion.104 = f32[64,128]{1,0:T(8,128)S(1)} fusion(s32[64,128]{1,0:T(8,128)S(1)} %dynamic-slice_bitcast_fusion.6, bf16[16,64,16,128]{3,2,1,0:T(8,128)(2,1)} %get-tuple-element.200, s32[]{:T(128)S(6)} %copy.98, f32[16,512]{1,0:T(8,128)S(1)} %get-tuple-element.202), kind=kOutput, calls=%fused_computation.5.clone.1 | convolution fusion | flops 809885696 | bytes 360452 | tf_op jit(solution)/shard_map/while/body/eval_jaxpr/ac,cgp->gap/dot_general | solution.py:147
  170.1 6.3 %fusion.104 = f32[64,128]{1,0:T(8,128)S(1)} fusion(s32[64,128]{1,0:T(8,128)S(1)} %dynamic-slice_bitcast_fusion.6, bf16[16,64,16,128]{3,2,1,0:T(8,128)(2,1)} %get-tuple-element.200, s32[]{:T(128)S(6)} %copy.98, f32[16,512]{1,0:T(8,128)S(1)} %get-tuple-element.202), kind=kOutput, calls=%fused_computation.5.clone.1 | convolution fusion | flops 809885696 | bytes 360452 | tf_op jit(solution)/shard_map/while/body/eval_jaxpr/ac,cgp->gap/dot_general | solution.py:147
  177.9 6.3 %fusion.104 = f32[64,128]{1,0:T(8,128)S(1)} fusion(s32[64,128]{1,0:T(8,128)S(1)} %dynamic-slice_bitcast_fusion.6, bf16[16,64,16,128]{3,2,1,0:T(8,128)(2,1)} %get-tuple-element.200, s32[]{:T(128)S(6)} %copy.98, f32[16,512]{1,0:T(8,128)S(1)} %get-tuple-element.202), kind=kOutput, calls=%fused_computation.5.clone.1 | convolution fusion | flops 809885696 | bytes 360452 | tf_op jit(solution)/shard_map/while/body/eval_jaxpr/ac,cgp->gap/dot_general | solution.py:147
  185.6 6.3 %fusion.104 = f32[64,128]{1,0:T(8,128)S(1)} fusion(s32[64,128]{1,0:T(8,128)S(1)} %dynamic-slice_bitcast_fusion.6, bf16[16,64,16,128]{3,2,1,0:T(8,128)(2,1)} %get-tuple-element.200, s32[]{:T(128)S(6)} %copy.98, f32[16,512]{1,0:T(8,128)S(1)} %get-tuple-element.202), kind=kOutput, calls=%fused_computation.5.clone.1 | convolution fusion | flops 809885696 | bytes 360452 | tf_op jit(solution)/shard_map/while/body/eval_jaxpr/ac,cgp->gap/dot_general | solution.py:147
  193.3 6.3 %fusion.104 = f32[64,128]{1,0:T(8,128)S(1)} fusion(s32[64,128]{1,0:T(8,128)S(1)} %dynamic-slice_bitcast_fusion.6, bf16[16,64,16,128]{3,2,1,0:T(8,128)(2,1)} %get-tuple-element.200, s32[]{:T(128)S(6)} %copy.98, f32[16,512]{1,0:T(8,128)S(1)} %get-tuple-element.202), kind=kOutput, calls=%fused_computation.5.clone.1 | convolution fusion | flops 809885696 | bytes 360452 | tf_op jit(solution)/shard_map/while/body/eval_jaxpr/ac,cgp->gap/dot_general | solution.py:147
  201.0 6.3 %fusion.104 = f32[64,128]{1,0:T(8,128)S(1)} fusion(s32[64,128]{1,0:T(8,128)S(1)} %dynamic-slice_bitcast_fusion.6, bf16[16,64,16,128]{3,2,1,0:T(8,128)(2,1)} %get-tuple-element.200, s32[]{:T(128)S(6)} %copy.98, f32[16,512]{1,0:T(8,128)S(1)} %get-tuple-element.202), kind=kOutput, calls=%fused_computation.5.clone.1 | convolution fusion | flops 809885696 | bytes 360452 | tf_op jit(solution)/shard_map/while/body/eval_jaxpr/ac,cgp->gap/dot_general | solution.py:147
  208.7 6.3 %fusion.104 = f32[64,128]{1,0:T(8,128)S(1)} fusion(s32[64,128]{1,0:T(8,128)S(1)} %dynamic-slice_bitcast_fusion.6, bf16[16,64,16,128]{3,2,1,0:T(8,128)(2,1)} %get-tuple-element.200, s32[]{:T(128)S(6)} %copy.98, f32[16,512]{1,0:T(8,128)S(1)} %get-tuple-element.202), kind=kOutput, calls=%fused_computation.5.clone.1 | convolution fusion | flops 809885696 | bytes 360452 | tf_op jit(solution)/shard_map/while/body/eval_jaxpr/ac,cgp->gap/dot_general | solution.py:147
  216.4 6.3 %fusion.104 = f32[64,128]{1,0:T(8,128)S(1)} fusion(s32[64,128]{1,0:T(8,128)S(1)} %dynamic-slice_bitcast_fusion.6, bf16[16,64,16,128]{3,2,1,0:T(8,128)(2,1)} %get-tuple-element.200, s32[]{:T(128)S(6)} %copy.98, f32[16,512]{1,0:T(8,128)S(1)} %get-tuple-element.202), kind=kOutput, calls=%fused_computation.5.clone.1 | convolution fusion | flops 809885696 | bytes 360452 | tf_op jit(solution)/shard_map/while/body/eval_jaxpr/ac,cgp->gap/dot_general | solution.py:147
  224.1 6.3 %fusion.104 = f32[64,128]{1,0:T(8,128)S(1)} fusion(s32[64,128]{1,0:T(8,128)S(1)} %dynamic-slice_bitcast_fusion.6, bf16[16,64,16,128]{3,2,1,0:T(8,128)(2,1)} %get-tuple-element.200, s32[]{:T(128)S(6)} %copy.98, f32[16,512]{1,0:T(8,128)S(1)} %get-tuple-element.202), kind=kOutput, calls=%fused_computation.5.clone.1 | convolution fusion | flops 809885696 | bytes 360452 | tf_op jit(solution)/shard_map/while/body/eval_jaxpr/ac,cgp->gap/dot_general | solution.py:147
  231.8 6.3 %fusion.104 = f32[64,128]{1,0:T(8,128)S(1)} fusion(s32[64,128]{1,0:T(8,128)S(1)} %dynamic-slice_bitcast_fusion.6, bf16[16,64,16,128]{3,2,1,0:T(8,128)(2,1)} %get-tuple-element.200, s32[]{:T(128)S(6)} %copy.98, f32[16,512]{1,0:T(8,128)S(1)} %get-tuple-element.202), kind=kOutput, calls=%fused_computation.5.clone.1 | convolution fusion | flops 809885696 | bytes 360452 | tf_op jit(solution)/shard_map/while/body/eval_jaxpr/ac,cgp->gap/dot_general | solution.py:147
  239.5 6.3 %fusion.104 = f32[64,128]{1,0:T(8,128)S(1)} fusion(s32[64,128]{1,0:T(8,128)S(1)} %dynamic-slice_bitcast_fusion.6, bf16[16,64,16,128]{3,2,1,0:T(8,128)(2,1)} %get-tuple-element.200, s32[]{:T(128)S(6)} %copy.98, f32[16,512]{1,0:T(8,128)S(1)} %get-tuple-element.202), kind=kOutput, calls=%fused_computation.5.clone.1 | convolution fusion | flops 809885696 | bytes 360452 | tf_op jit(solution)/shard_map/while/body/eval_jaxpr/ac,cgp->gap/dot_general | solution.py:147
  247.2 6.3 %fusion.104 = f32[64,128]{1,0:T(8,128)S(1)} fusion(s32[64,128]{1,0:T(8,128)S(1)} %dynamic-slice_bitcast_fusion.6, bf16[16,64,16,128]{3,2,1,0:T(8,128)(2,1)} %get-tuple-element.200, s32[]{:T(128)S(6)} %copy.98, f32[16,512]{1,0:T(8,128)S(1)} %get-tuple-element.202), kind=kOutput, calls=%fused_computation.5.clone.1 | convolution fusion | flops 809885696 | bytes 360452 | tf_op jit(solution)/shard_map/while/body/eval_jaxpr/ac,cgp->gap/dot_general | solution.py:147
  254.9 6.3 %fusion.104 = f32[64,128]{1,0:T(8,128)S(1)} fusion(s32[64,128]{1,0:T(8,128)S(1)} %dynamic-slice_bitcast_fusion.6, bf16[16,64,16,128]{3,2,1,0:T(8,128)(2,1)} %get-tuple-element.200, s32[]{:T(128)S(6)} %copy.98, f32[16,512]{1,0:T(8,128)S(1)} %get-tuple-element.202), kind=kOutput, calls=%fused_computation.5.clone.1 | convolution fusion | flops 809885696 | bytes 360452 | tf_op jit(solution)/shard_map/while/body/eval_jaxpr/ac,cgp->gap/dot_general | solution.py:147
  262.6 6.3 %fusion.104 = f32[64,128]{1,0:T(8,128)S(1)} fusion(s32[64,128]{1,0:T(8,128)S(1)} %dynamic-slice_bitcast_fusion.6, bf16[16,64,16,128]{3,2,1,0:T(8,128)(2,1)} %get-tuple-element.200, s32[]{:T(128)S(6)} %copy.98, f32[16,512]{1,0:T(8,128)S(1)} %get-tuple-element.202), kind=kOutput, calls=%fused_computation.5.clone.1 | convolution fusion | flops 809885696 | bytes 360452 | tf_op jit(solution)/shard_map/while/body/eval_jaxpr/ac,cgp->gap/dot_general | solution.py:147
  270.3 6.3 %fusion.104 = f32[64,128]{1,0:T(8,128)S(1)} fusion(s32[64,128]{1,0:T(8,128)S(1)} %dynamic-slice_bitcast_fusion.6, bf16[16,64,16,128]{3,2,1,0:T(8,128)(2,1)} %get-tuple-element.200, s32[]{:T(128)S(6)} %copy.98, f32[16,512]{1,0:T(8,128)S(1)} %get-tuple-element.202), kind=kOutput, calls=%fused_computation.5.clone.1 | convolution fusion | flops 809885696 | bytes 360452 | tf_op jit(solution)/shard_map/while/body/eval_jaxpr/ac,cgp->gap/dot_general | solution.py:147
  277.3 5.8 %all-to-all-start.1 = ((s32[8,128,1]{1,2,0:T(1,128)}), s32[8,128,1]{1,2,0:T(1,128)S(1)}, u32[]{:S(2)}, u32[]{:S(2)}) async-start(s32[8,128,1]{1,2,0:T(1,128)} %slice_bitcast_fusion.1), calls=%async_computation.1 | async-start | bytes 8192 | tf_op jit(solution)/shard_map/all_to_all | solution.py:137
  283.1 1.5 fusion.94
  284.6 4.9 all-to-all-done.1
  289.5 22.2 %all-reduce.2.cloned.1.call-done = f32[1024,128]{1,0:T(8,128)} async-done(((f32[1024,128]{1,0:T(8,128)}), f32[1024,128]{1,0:T(8,128)}) %all-reduce.2.cloned.1.call-update) | async-done | bytes 524304 | tf_op jit(solution)/shard_map/psum | solution.py:153
  311.7 1.4 fusion.74
  313.1 147.6 %while.22 = (s32[]{:T(128)}, f32[16,512]{1,0:T(8,128)S(1)}, bf16[16,64,16,128]{3,2,1,0:T(8,128)(2,1)}, f32[16,64,128]{2,1,0:T(8,128)S(1)}, s32[16,64,128]{2,1,0:T(8,128)}, /*index=5*/s32[]{:T(128)}, s32[]{:T(128)}) while((s32[]{:T(128)}, f32[16,512]{1,0:T(8,128)S(1)}, bf16[16,64,16,128]{3,2,1,0:T(8,128)(2,1)}, ...), condition=%wide.region_8.9_spmd.clone, body=%wide.region_7.8_spmd.clone.sunk | while | flops 809779200 | bytes 524395 | solution.py:166
  313.9 8.4 %fusion.105 = f32[16,512]{1,0:T(8,128)S(1)} fusion(s32[64,128]{1,0:T(8,128)S(1)} %dynamic-slice_bitcast_fusion.7, f32[64,128]{1,0:T(8,128)S(1)} %dynamic-slice_bitcast_fusion.8, bf16[16,64,16,128]{3,2,1,0:T(8,128)(2,1)} %get-tuple-element.220, s32[]{:T(128)S(6)} %copy.105, f32[16,512]{1,0:T(8,128)S(1)} %get-tuple-element.212, pred[]{:T(512)S(6)} %compare.3), kind=kOutput, calls=%fused_computation.13.clone.1 | convolution fusion | flops 809779200 | bytes 393221 | tf_op jit(solution)/shard_map/while/body/eval_jaxpr/gap,cgp->ac/dot_general | solution.py:162
  323.2 8.4 %fusion.105 = f32[16,512]{1,0:T(8,128)S(1)} fusion(s32[64,128]{1,0:T(8,128)S(1)} %dynamic-slice_bitcast_fusion.7, f32[64,128]{1,0:T(8,128)S(1)} %dynamic-slice_bitcast_fusion.8, bf16[16,64,16,128]{3,2,1,0:T(8,128)(2,1)} %get-tuple-element.220, s32[]{:T(128)S(6)} %copy.105, f32[16,512]{1,0:T(8,128)S(1)} %get-tuple-element.212, pred[]{:T(512)S(6)} %compare.3), kind=kOutput, calls=%fused_computation.13.clone.1 | convolution fusion | flops 809779200 | bytes 393221 | tf_op jit(solution)/shard_map/while/body/eval_jaxpr/gap,cgp->ac/dot_general | solution.py:162
  332.4 8.4 %fusion.105 = f32[16,512]{1,0:T(8,128)S(1)} fusion(s32[64,128]{1,0:T(8,128)S(1)} %dynamic-slice_bitcast_fusion.7, f32[64,128]{1,0:T(8,128)S(1)} %dynamic-slice_bitcast_fusion.8, bf16[16,64,16,128]{3,2,1,0:T(8,128)(2,1)} %get-tuple-element.220, s32[]{:T(128)S(6)} %copy.105, f32[16,512]{1,0:T(8,128)S(1)} %get-tuple-element.212, pred[]{:T(512)S(6)} %compare.3), kind=kOutput, calls=%fused_computation.13.clone.1 | convolution fusion | flops 809779200 | bytes 393221 | tf_op jit(solution)/shard_map/while/body/eval_jaxpr/gap,cgp->ac/dot_general | solution.py:162
  341.6 8.4 %fusion.105 = f32[16,512]{1,0:T(8,128)S(1)} fusion(s32[64,128]{1,0:T(8,128)S(1)} %dynamic-slice_bitcast_fusion.7, f32[64,128]{1,0:T(8,128)S(1)} %dynamic-slice_bitcast_fusion.8, bf16[16,64,16,128]{3,2,1,0:T(8,128)(2,1)} %get-tuple-element.220, s32[]{:T(128)S(6)} %copy.105, f32[16,512]{1,0:T(8,128)S(1)} %get-tuple-element.212, pred[]{:T(512)S(6)} %compare.3), kind=kOutput, calls=%fused_computation.13.clone.1 | convolution fusion | flops 809779200 | bytes 393221 | tf_op jit(solution)/shard_map/while/body/eval_jaxpr/gap,cgp->ac/dot_general | solution.py:162
  350.8 8.4 %fusion.105 = f32[16,512]{1,0:T(8,128)S(1)} fusion(s32[64,128]{1,0:T(8,128)S(1)} %dynamic-slice_bitcast_fusion.7, f32[64,128]{1,0:T(8,128)S(1)} %dynamic-slice_bitcast_fusion.8, bf16[16,64,16,128]{3,2,1,0:T(8,128)(2,1)} %get-tuple-element.220, s32[]{:T(128)S(6)} %copy.105, f32[16,512]{1,0:T(8,128)S(1)} %get-tuple-element.212, pred[]{:T(512)S(6)} %compare.3), kind=kOutput, calls=%fused_computation.13.clone.1 | convolution fusion | flops 809779200 | bytes 393221 | tf_op jit(solution)/shard_map/while/body/eval_jaxpr/gap,cgp->ac/dot_general | solution.py:162
  360.1 8.4 %fusion.105 = f32[16,512]{1,0:T(8,128)S(1)} fusion(s32[64,128]{1,0:T(8,128)S(1)} %dynamic-slice_bitcast_fusion.7, f32[64,128]{1,0:T(8,128)S(1)} %dynamic-slice_bitcast_fusion.8, bf16[16,64,16,128]{3,2,1,0:T(8,128)(2,1)} %get-tuple-element.220, s32[]{:T(128)S(6)} %copy.105, f32[16,512]{1,0:T(8,128)S(1)} %get-tuple-element.212, pred[]{:T(512)S(6)} %compare.3), kind=kOutput, calls=%fused_computation.13.clone.1 | convolution fusion | flops 809779200 | bytes 393221 | tf_op jit(solution)/shard_map/while/body/eval_jaxpr/gap,cgp->ac/dot_general | solution.py:162
  369.3 8.4 %fusion.105 = f32[16,512]{1,0:T(8,128)S(1)} fusion(s32[64,128]{1,0:T(8,128)S(1)} %dynamic-slice_bitcast_fusion.7, f32[64,128]{1,0:T(8,128)S(1)} %dynamic-slice_bitcast_fusion.8, bf16[16,64,16,128]{3,2,1,0:T(8,128)(2,1)} %get-tuple-element.220, s32[]{:T(128)S(6)} %copy.105, f32[16,512]{1,0:T(8,128)S(1)} %get-tuple-element.212, pred[]{:T(512)S(6)} %compare.3), kind=kOutput, calls=%fused_computation.13.clone.1 | convolution fusion | flops 809779200 | bytes 393221 | tf_op jit(solution)/shard_map/while/body/eval_jaxpr/gap,cgp->ac/dot_general | solution.py:162
  378.5 8.4 %fusion.105 = f32[16,512]{1,0:T(8,128)S(1)} fusion(s32[64,128]{1,0:T(8,128)S(1)} %dynamic-slice_bitcast_fusion.7, f32[64,128]{1,0:T(8,128)S(1)} %dynamic-slice_bitcast_fusion.8, bf16[16,64,16,128]{3,2,1,0:T(8,128)(2,1)} %get-tuple-element.220, s32[]{:T(128)S(6)} %copy.105, f32[16,512]{1,0:T(8,128)S(1)} %get-tuple-element.212, pred[]{:T(512)S(6)} %compare.3), kind=kOutput, calls=%fused_computation.13.clone.1 | convolution fusion | flops 809779200 | bytes 393221 | tf_op jit(solution)/shard_map/while/body/eval_jaxpr/gap,cgp->ac/dot_general | solution.py:162
  387.7 8.4 %fusion.105 = f32[16,512]{1,0:T(8,128)S(1)} fusion(s32[64,128]{1,0:T(8,128)S(1)} %dynamic-slice_bitcast_fusion.7, f32[64,128]{1,0:T(8,128)S(1)} %dynamic-slice_bitcast_fusion.8, bf16[16,64,16,128]{3,2,1,0:T(8,128)(2,1)} %get-tuple-element.220, s32[]{:T(128)S(6)} %copy.105, f32[16,512]{1,0:T(8,128)S(1)} %get-tuple-element.212, pred[]{:T(512)S(6)} %compare.3), kind=kOutput, calls=%fused_computation.13.clone.1 | convolution fusion | flops 809779200 | bytes 393221 | tf_op jit(solution)/shard_map/while/body/eval_jaxpr/gap,cgp->ac/dot_general | solution.py:162
  397.0 8.4 %fusion.105 = f32[16,512]{1,0:T(8,128)S(1)} fusion(s32[64,128]{1,0:T(8,128)S(1)} %dynamic-slice_bitcast_fusion.7, f32[64,128]{1,0:T(8,128)S(1)} %dynamic-slice_bitcast_fusion.8, bf16[16,64,16,128]{3,2,1,0:T(8,128)(2,1)} %get-tuple-element.220, s32[]{:T(128)S(6)} %copy.105, f32[16,512]{1,0:T(8,128)S(1)} %get-tuple-element.212, pred[]{:T(512)S(6)} %compare.3), kind=kOutput, calls=%fused_computation.13.clone.1 | convolution fusion | flops 809779200 | bytes 393221 | tf_op jit(solution)/shard_map/while/body/eval_jaxpr/gap,cgp->ac/dot_general | solution.py:162
  406.2 8.4 %fusion.105 = f32[16,512]{1,0:T(8,128)S(1)} fusion(s32[64,128]{1,0:T(8,128)S(1)} %dynamic-slice_bitcast_fusion.7, f32[64,128]{1,0:T(8,128)S(1)} %dynamic-slice_bitcast_fusion.8, bf16[16,64,16,128]{3,2,1,0:T(8,128)(2,1)} %get-tuple-element.220, s32[]{:T(128)S(6)} %copy.105, f32[16,512]{1,0:T(8,128)S(1)} %get-tuple-element.212, pred[]{:T(512)S(6)} %compare.3), kind=kOutput, calls=%fused_computation.13.clone.1 | convolution fusion | flops 809779200 | bytes 393221 | tf_op jit(solution)/shard_map/while/body/eval_jaxpr/gap,cgp->ac/dot_general | solution.py:162
  415.4 8.4 %fusion.105 = f32[16,512]{1,0:T(8,128)S(1)} fusion(s32[64,128]{1,0:T(8,128)S(1)} %dynamic-slice_bitcast_fusion.7, f32[64,128]{1,0:T(8,128)S(1)} %dynamic-slice_bitcast_fusion.8, bf16[16,64,16,128]{3,2,1,0:T(8,128)(2,1)} %get-tuple-element.220, s32[]{:T(128)S(6)} %copy.105, f32[16,512]{1,0:T(8,128)S(1)} %get-tuple-element.212, pred[]{:T(512)S(6)} %compare.3), kind=kOutput, calls=%fused_computation.13.clone.1 | convolution fusion | flops 809779200 | bytes 393221 | tf_op jit(solution)/shard_map/while/body/eval_jaxpr/gap,cgp->ac/dot_general | solution.py:162
  424.7 8.4 %fusion.105 = f32[16,512]{1,0:T(8,128)S(1)} fusion(s32[64,128]{1,0:T(8,128)S(1)} %dynamic-slice_bitcast_fusion.7, f32[64,128]{1,0:T(8,128)S(1)} %dynamic-slice_bitcast_fusion.8, bf16[16,64,16,128]{3,2,1,0:T(8,128)(2,1)} %get-tuple-element.220, s32[]{:T(128)S(6)} %copy.105, f32[16,512]{1,0:T(8,128)S(1)} %get-tuple-element.212, pred[]{:T(512)S(6)} %compare.3), kind=kOutput, calls=%fused_computation.13.clone.1 | convolution fusion | flops 809779200 | bytes 393221 | tf_op jit(solution)/shard_map/while/body/eval_jaxpr/gap,cgp->ac/dot_general | solution.py:162
  433.9 8.4 %fusion.105 = f32[16,512]{1,0:T(8,128)S(1)} fusion(s32[64,128]{1,0:T(8,128)S(1)} %dynamic-slice_bitcast_fusion.7, f32[64,128]{1,0:T(8,128)S(1)} %dynamic-slice_bitcast_fusion.8, bf16[16,64,16,128]{3,2,1,0:T(8,128)(2,1)} %get-tuple-element.220, s32[]{:T(128)S(6)} %copy.105, f32[16,512]{1,0:T(8,128)S(1)} %get-tuple-element.212, pred[]{:T(512)S(6)} %compare.3), kind=kOutput, calls=%fused_computation.13.clone.1 | convolution fusion | flops 809779200 | bytes 393221 | tf_op jit(solution)/shard_map/while/body/eval_jaxpr/gap,cgp->ac/dot_general | solution.py:162
  443.1 8.4 %fusion.105 = f32[16,512]{1,0:T(8,128)S(1)} fusion(s32[64,128]{1,0:T(8,128)S(1)} %dynamic-slice_bitcast_fusion.7, f32[64,128]{1,0:T(8,128)S(1)} %dynamic-slice_bitcast_fusion.8, bf16[16,64,16,128]{3,2,1,0:T(8,128)(2,1)} %get-tuple-element.220, s32[]{:T(128)S(6)} %copy.105, f32[16,512]{1,0:T(8,128)S(1)} %get-tuple-element.212, pred[]{:T(512)S(6)} %compare.3), kind=kOutput, calls=%fused_computation.13.clone.1 | convolution fusion | flops 809779200 | bytes 393221 | tf_op jit(solution)/shard_map/while/body/eval_jaxpr/gap,cgp->ac/dot_general | solution.py:162
  452.3 8.4 %fusion.105 = f32[16,512]{1,0:T(8,128)S(1)} fusion(s32[64,128]{1,0:T(8,128)S(1)} %dynamic-slice_bitcast_fusion.7, f32[64,128]{1,0:T(8,128)S(1)} %dynamic-slice_bitcast_fusion.8, bf16[16,64,16,128]{3,2,1,0:T(8,128)(2,1)} %get-tuple-element.220, s32[]{:T(128)S(6)} %copy.105, f32[16,512]{1,0:T(8,128)S(1)} %get-tuple-element.212, pred[]{:T(512)S(6)} %compare.3), kind=kOutput, calls=%fused_computation.13.clone.1 | convolution fusion | flops 809779200 | bytes 393221 | tf_op jit(solution)/shard_map/while/body/eval_jaxpr/gap,cgp->ac/dot_general | solution.py:162
  463.0 5.3 %collective-permute-start.2 = (f32[16,32,4]{2,0,1:T(8,128)S(1)}, f32[16,32,4]{2,0,1:T(8,128)}, u32[]{:S(2)}, u32[]{:S(2)}) collective-permute-start(f32[16,32,4]{2,0,1:T(8,128)S(1)} %get-tuple-element.105), channel_id=1, source_target_pairs={{0,4},{4,8},{8,12},{12,16},{16,20},{20,24},{24,28},{1,5},{5,9},{9,... | collective-permute-start | bytes 24584 | tf_op jit(solution)/shard_map/ppermute | solution.py:18
  468.9 1.9 collective-permute-done.3
  470.8 5.7 %collective-permute-done.2 = f32[16,32,4]{2,0,1:T(8,128)} collective-permute-done((f32[16,32,4]{2,0,1:T(8,128)S(1)}, f32[16,32,4]{2,0,1:T(8,128)}, u32[]{:S(2)}, u32[]{:S(2)}) %collective-permute-start.2) | collective-permute-done | bytes 8224 | tf_op jit(solution)/shard_map/ppermute | solution.py:18
  476.5 10.4 %fusion.25 = bf16[16,32,512]{2,0,1:T(8,128)(2,1)} fusion(f32[16,32,512]{2,0,1:T(8,128)S(1)} %fusion.71, f32[16,32,4]{2,0,1:T(8,128)} %collective-permute-done.3, f32[16,32,4]{2,0,1:T(8,128)} %collective-permute-done.2, f32[16,1,32,512]{3,0,2,1:T(8,128)S(1)} %get-tuple-element.100, f32[]{:T(128)S(6)} %mul.235, f32[16,512]{1,0:T(8,128)S(1)} %get-tuple-element.60, ...), kind=kLoop, calls=%fused_computation.60 | loop fusion | flops 7077888 | bytes 2670628 | tf_op jit(solution)/shard_map/convert_element_type | solution.py:172
  486.9 23.0 %all-gather.5.cloned.1.call-done = bf16[64,32,512]{2,0,1:T(8,128)(2,1)} async-done(((bf16[16,32,512]{2,0,1:T(8,128)(2,1)}), bf16[64,32,512]{2,0,1:T(8,128)(2,1)}) %all-gather.5.cloned.1.call-update) | async-done | bytes 2097168 | tf_op jit(solution)/shard_map/all_gather | solution.py:177
  509.8 2.5 convolution_add_fusion
  512.3 1.6 copy.65
  (113 shorter events, 47.5 us)
Async XLA Ops:
  6.5 13.2 %copy-start.9 = (bf16[512,16,128]{2,1,0:T(8,128)(2,1)S(1)}, bf16[512,16,128]{2,1,0:T(8,128)(2,1)}, u32[]{:S(2)}) copy-start(bf16[512,16,128]{2,1,0:T(8,128)(2,1)} %param.16) | copy-start | bytes 6291460
  11.5 1.0 copy-start.5
  12.4 21.8 %all-to-all-start.3 = ((s32[8,128,128]{1,2,0:T(8,128)}), s32[8,128,128]{1,2,0:T(8,128)S(1)}, u32[]{:S(2)}, u32[]{:S(2)}) async-start(s32[8,128,128]{1,2,0:T(8,128)} %copy_bitcast_fusion), calls=%async_computation.3 | async-start | bytes 1048576 | tf_op jit(solution)/shard_map/all_to_all | solution.py:136
  34.2 0.8 copy-start.2
  35.0 4.8 copy-start
  35.0 6.2 %copy-start.6 = (bf16[512,128]{1,0:T(8,128)(2,1)S(1)}, bf16[512,128]{1,0:T(8,128)(2,1)}, u32[]{:S(2)}) copy-start(bf16[512,128]{1,0:T(8,128)(2,1)} %param.18) | copy-start | bytes 393220
  35.0 99.3 %all-to-all-start = ((bf16[1024,16,128]{2,1,0:T(8,128)(2,1)}), bf16[1024,16,128]{2,1,0:T(8,128)(2,1)}, u32[]{:S(2)}, u32[]{:S(2)}) async-start(bf16[1024,16,128]{2,1,0:T(8,128)(2,1)} %bitcast.110), calls=%async_computation | async-start | bytes 8388608 | tf_op jit(solution)/shard_map/all_to_all | solution.py:132
  39.7 1.7 copy-start.7
  39.7 6.6 %copy-start.1 = (bf16[16,4,32,512]{3,2,1,0:T(8,128)(2,1)S(1)}, bf16[16,4,32,512]{3,2,1,0:T(8,128)(2,1)}, u32[]{:S(2)}) copy-start(bf16[16,4,32,512]{3,2,1,0:T(8,128)(2,1)} %param.14) | copy-start | bytes 6291460
  39.7 26.3 %all-gather.3.cloned.1.call-start = ((), (), s32[]{:S(2)}) async-start(), calls=%async_computation.4 | async-start | bytes 2621440 | tf_op jit(solution)/shard_map/all_gather | solution.py:91
  47.7 27.7 %copy-start.8 = (f32[4]{0:T(128)S(1)}, f32[4]{0:T(128)}, u32[]{:S(2)}) copy-start(f32[4]{0:T(128)} %param.15) | copy-start | bytes 52
  47.7 28.3 %copy-start.4 = (bf16[1024,256]{0,1:T(8,128)(2,1)S(1)}, bf16[1024,256]{0,1:T(8,128)(2,1)}, u32[]{:S(2)}) copy-start(bf16[1024,256]{0,1:T(8,128)(2,1)} %fusion.18) | copy-start | bytes 1572868
  47.7 29.4 %copy-start.3 = (s32[8,128,128]{1,2,0:T(8,128)S(1)}, s32[8,128,128]{1,2,0:T(8,128)}, u32[]{:S(2)}) copy-start(s32[8,128,128]{1,2,0:T(8,128)} %copy-done.2) | copy-start | bytes 1572868
  68.8 21.6 %collective-permute-start.1 = (f32[16,32,4]{2,0,1:T(8,128)}, f32[16,32,4]{2,0,1:T(8,128)}, u32[]{:S(2)}, u32[]{:S(2)}) collective-permute-start(f32[16,32,4]{2,0,1:T(8,128)} %get-tuple-element.108), channel_id=1, source_target_pairs={{4,0},{8,4},{12,8},{16,12},{20,16},{24,20},{28,24},{5,1},{9,5},{13... | collective-permute-start | bytes 24584 | tf_op jit(solution)/shard_map/ppermute | solution.py:19
  70.1 20.3 %collective-permute-start = (f32[16,32,4]{2,0,1:T(8,128)S(1)}, f32[16,32,4]{2,0,1:T(8,128)}, u32[]{:S(2)}, u32[]{:S(2)}) collective-permute-start(f32[16,32,4]{2,0,1:T(8,128)S(1)} %get-tuple-element.107), channel_id=1, source_target_pairs={{0,4},{4,8},{8,12},{12,16},{16,20},{20,24},{24,28},{1,5},{5,9},{9,... | collective-permute-start | bytes 24584 | tf_op jit(solution)/shard_map/ppermute | solution.py:18
  134.3 143.0 %all-to-all-start.2 = ((bf16[1024,2,128]{2,1,0:T(2,128)(2,1)}), bf16[1024,2,128]{2,1,0:T(2,128)(2,1)S(1)}, u32[]{:S(2)}, u32[]{:S(2)}) async-start(bf16[1024,2,128]{2,1,0:T(2,128)(2,1)} %copy.58), calls=%async_computation.2 | async-start | bytes 1048576 | tf_op jit(solution)/shard_map/all_to_all | solution.py:133
  153.7 158.0 %all-reduce.2.cloned.1.call-start = ((), (), s32[]{:S(2)}) async-start(), calls=%async_computation.5 | async-start | bytes 1048576 | tf_op jit(solution)/shard_map/psum | solution.py:153
  277.3 12.2 %all-to-all-start.1 = ((s32[8,128,1]{1,2,0:T(1,128)}), s32[8,128,1]{1,2,0:T(1,128)S(1)}, u32[]{:S(2)}, u32[]{:S(2)}) async-start(s32[8,128,1]{1,2,0:T(1,128)} %slice_bitcast_fusion.1), calls=%async_computation.1 | async-start | bytes 8192 | tf_op jit(solution)/shard_map/all_to_all | solution.py:137
  283.1 226.8 %all-gather.5.cloned.1.call-start = ((), (), s32[]{:S(2)}) async-start(), calls=%async_computation.6 | async-start | bytes 2621440 | tf_op jit(solution)/shard_map/all_gather | solution.py:177
  461.8 9.1 %collective-permute-start.3 = (f32[16,32,4]{2,0,1:T(8,128)}, f32[16,32,4]{2,0,1:T(8,128)}, u32[]{:S(2)}, u32[]{:S(2)}) collective-permute-start(f32[16,32,4]{2,0,1:T(8,128)} %get-tuple-element.106), channel_id=1, source_target_pairs={{4,0},{8,4},{12,8},{16,12},{20,16},{24,20},{28,24},{5,1},{9,5},{13... | collective-permute-start | bytes 24584 | tf_op jit(solution)/shard_map/ppermute | solution.py:19
  463.0 13.4 %collective-permute-start.2 = (f32[16,32,4]{2,0,1:T(8,128)S(1)}, f32[16,32,4]{2,0,1:T(8,128)}, u32[]{:S(2)}, u32[]{:S(2)}) collective-permute-start(f32[16,32,4]{2,0,1:T(8,128)S(1)} %get-tuple-element.105), channel_id=1, source_target_pairs={{0,4},{4,8},{8,12},{12,16},{16,20},{20,24},{24,28},{1,5},{5,9},{9,... | collective-permute-start | bytes 24584 | tf_op jit(solution)/shard_map/ppermute | solution.py:18
Sparse Core Ops, SparseCore 0:
  42.1 23.8 all-gather.2
  277.4 34.3 all-reduce.1
  487.0 22.7 all-gather.4
where the time goes:
time: 525 us; the launch traced here: 520 us
  matrix products  248 us (47%)
  waiting for transfers between devices  128 us (24%)
  local copies, waits for them, and re-layouts  51.6 us (10%)
  starting transfers between devices  50.5 us (10%)
  other arithmetic  28.7 us (5%)
  between operations  14 us (3%)
    dot_general x16, matrix products, adjoint_group(): jnp.einsum('gap,cgp->ac', contrib, onehot, precision=lax.Precision.HIGHEST)  135 us
    dot_general x16, matrix products, forward_group(): jnp.einsum('ac,cgp->gap', column_field, onehot, precision=lax.Precision.H...  101 us
    all_to_all x1, waiting for transfers between devices, body(): lax.all_to_all(kernel_buf, 'horiz', split_axis=0, concat_axis=0, tiled=True)  30.8 us
    eq x32, local copies, waits for them, and re-layouts, column_onehot(): jnp.arange(col_count, dtype=jnp.int32)[:, None, None]  24.7 us
    all_gather x1, waiting for transfers between devices, body(): lax.all_gather(smoothed_b, 'lev', axis=0, tiled=True)  23 us
    psum x1, waiting for transfers between devices, body(): evolved = lax.psum(local_sums, 'lev')  22.2 us
    all_to_all x1, starting transfers between devices, body(): lax.all_to_all(value_buf, 'horiz', split_axis=0, concat_axis=0, tiled=True)  19.4 us
    all_gather x1, waiting for transfers between devices, body(): lax.all_gather(control_b, 'lev', axis=0, tiled=True)  18.3 us
  transfers between devices with their start and end apart: 11, of which 9 were waited for; matrix products, arithmetic and copies ran while one was open for 30% of the time, Pallas kernels for 0%

commit v1 on v0

--- a/solution.py
+++ b/solution.py
@@ -6,6 +6,29 @@
 
 LEV = 64
 HALF = 4
+
+
+def split_up(shard, dim, devices):
+    dims = shard.shape
+    pieces = shard.reshape(*dims[:dim], devices, dims[dim] // devices, *dims[dim + 1 :])
+    return jnp.moveaxis(pieces, dim, 0)
+
+
+def laid_out(blocks, dim):
+    shape = list(blocks.shape[1:])
+    shape[dim] *= blocks.shape[0]
+    return jnp.moveaxis(blocks, 0, dim).reshape(shape)
+
+
+def exchange_in_pairs(value, axis, split_dim, concat_dim):
+    size, mine = (lax.axis_size(axis), lax.axis_index(axis))
+    blocks = split_up(value, split_dim, size)
+    outs = [blocks[mine]]
+    for step in range(1, size):
+        sent = blocks[mine ^ step]
+        outs.append(lax.ppermute(sent, axis, [(i, i ^ step) for i in range(size)]))
+    blocks = jnp.stack(outs)[mine ^ jnp.arange(size)]
+    return laid_out(blocks, concat_dim)
 
 
 def with_halo(value, sides, width):
@@ -133,7 +156,7 @@
         lax.all_to_all(value_buf, "horiz", split_axis=0, concat_axis=0, tiled=True),
     )
     column_in, count_in = (
-        lax.all_to_all(column_buf, "horiz", split_axis=0, concat_axis=0, tiled=True),
+        exchange_in_pairs(column_buf, "horiz", 0, 0),
         lax.all_to_all(count_buf, "horiz", split_axis=0, concat_axis=0, tiled=True),
     )
     slot_group = math.gcd(total_slots, 64)

time: 525 us -> 533 us (1.015)
  local copies, waits for them, and re-layouts: 51.6 us -> 69.2 us
  starting transfers between devices: 50.5 us -> 44.8 us
    ppermute x0 -> x7, waiting for transfers between devices: none -> 62.4 us  [exchange_in_pairs(): outs.append(lax.ppermute(sent, axis, [(i, i ^ step) for i in range(size)]))]
    all_to_all x1, waiting for transfers between devices: 30.8 us -> 0.01 us  [body(): lax.all_to_all(kernel_buf, 'horiz', split_axis=0, concat_axis=0, tiled=True)]
    all_gather x1, waiting for transfers between devices: 18.3 us -> 0.01 us  [body(): lax.all_gather(control_b, 'lev', axis=0, tiled=True)]
    all_to_all x1, starting transfers between devices: 19.4 us -> 4.63 us  [body(): lax.all_to_all(value_buf, 'horiz', split_axis=0, concat_axis=0, tiled=True)]
    ppermute x0 -> x7, starting transfers between devices: none -> 14.3 us  [exchange_in_pairs(): outs.append(lax.ppermute(sent, axis, [(i, i ^ step) for i in range(size)]))]
    ppermute x2, waiting for transfers between devices: 14.1 us -> 1.95 us  [with_halo(): after = lax.ppermute(first, axis, down)]
    unnamed x24 -> x32, local copies, waits for them, and re-layouts: 5.98 us -> 17.2 us
    all_to_all x1 -> x0, waiting for transfers between devices: 8.7 us -> none  [body(): lax.all_to_all(column_buf, 'horiz', split_axis=0, concat_axis=0, tiled=True)]
  transfers between devices with their start and end apart: 11 -> 17, of which waited for: 9 -> 10; matrix products, arithmetic and copies ran while one was open for 30% -> 32% of each run, Pallas kernels for 0% -> 0%
where the time goes in v1:
time: 533 us; the launch traced here: 529 us
  matrix products  248 us (47%)
  waiting for transfers between devices  124 us (23%)
  local copies, waits for them, and re-layouts  69.2 us (13%)
  starting transfers between devices  44.8 us (8%)
  other arithmetic  28.1 us (5%)
  between operations  14 us (3%)
    dot_general x16, matrix products, adjoint_group(): jnp.einsum('gap,cgp->ac', contrib, onehot, precision=lax.Precision.HIGHEST)  135 us
    dot_general x16, matrix products, forward_group(): jnp.einsum('ac,cgp->gap', column_field, onehot, precision=lax.Precision.H...  101 us
    ppermute x7, waiting for transfers between devices, exchange_in_pairs(): outs.append(lax.ppermute(sent, axis, [(i, i ^ step) for i in range(size)]))  62.4 us
    eq x32, local copies, waits for them, and re-layouts, column_onehot(): jnp.arange(col_count, dtype=jnp.int32)[:, None, None]  24.7 us
    all_gather x1, waiting for transfers between devices, body(): lax.all_gather(smoothed_b, 'lev', axis=0, tiled=True)  23 us
    psum x1, waiting for transfers between devices, body(): evolved = lax.psum(local_sums, 'lev')  22.3 us
    unnamed x32, local copies, waits for them, and re-layouts  17.2 us
    ppermute x7, starting transfers between devices, exchange_in_pairs(): outs.append(lax.ppermute(sent, axis, [(i, i ^ step) for i in range(size)]))  14.3 us
  transfers between devices with their start and end apart: 17, of which 10 were waited for; matrix products, arithmetic and copies ran while one was open for 32% of the time, Pallas kernels for 0%

profile of v1, /device:TPU:0, one launch (start us, length us, event | category | flops | bytes accessed | tf_op | source)
XLA Modules:
  0.0 528.6 jit_solution(10550397455923203279)
XLA Ops:
  8.2 3.9 convert_bitcast_fusion
  12.2 3.4 copy.73
  15.6 7.4 %all-to-all-start = ((bf16[1024,16,128]{2,1,0:T(8,128)(2,1)}), bf16[1024,16,128]{2,1,0:T(8,128)(2,1)}, u32[]{:S(2)}, u32[]{:S(2)}) async-start(bf16[1024,16,128]{2,1,0:T(8,128)(2,1)} %bitcast.133), calls=%async_computation | async-start | bytes 8388608 | tf_op jit(solution)/shard_map/all_to_all | solution.py:155
  28.2 2.0 collective-permute-start
  33.8 2.9 collective-permute-start.3
  44.0 2.0 copy.50
  52.0 7.0 %collective-permute-done = s32[128,128]{1,0:T(8,128)} collective-permute-done((s32[128,128]{1,0:T(8,128)}, s32[128,128]{1,0:T(8,128)}, u32[]{:S(2)}, u32[]{:S(2)}) %collective-permute-start) | collective-permute-done | bytes 65568 | tf_op jit(solution)/shard_map/ppermute | solution.py:29
  59.0 2.7 collective-permute-start.5
  63.1 31.2 %collective-permute-done.1 = s32[128,128]{1,0:T(8,128)} collective-permute-done((s32[128,128]{1,0:T(8,128)}, s32[128,128]{1,0:T(8,128)}, u32[]{:S(2)}, u32[]{:S(2)}) %collective-permute-start.1) | collective-permute-done | bytes 65568 | tf_op jit(solution)/shard_map/ppermute | solution.py:29
  94.4 3.7 collective-permute-start.6
  101.0 23.7 %collective-permute-done.3 = s32[128,128]{1,0:T(8,128)} collective-permute-done((s32[128,128]{1,0:T(8,128)}, s32[128,128]{1,0:T(8,128)}, u32[]{:S(2)}, u32[]{:S(2)}) %collective-permute-start.3) | collective-permute-done | bytes 65568 | tf_op jit(solution)/shard_map/ppermute | solution.py:29
  124.8 1.5 bitcast_dynamic-update-slice_fusion.4
  126.7 1.5 bitcast_dynamic-update-slice_fusion.3
  128.8 2.0 fusion.82
  132.3 4.6 collective-permute-start.7
  137.5 2.5 gather_fusion
  140.0 3.8 collective-permute-done.7
  144.5 12.7 %fusion.47 = (f32[16,512]{1,0:T(8,128)S(1)}, f32[16,1,32,512]{3,0,2,1:T(8,128)S(1)}) fusion(f32[16,32,512]{2,0,1:T(8,128)S(1)} %fusion.82, f32[16,32,4]{2,0,1:T(8,128)S(1)} %collective-permute-done.8, f32[16,32,4]{2,0,1:T(8,128)} %copy-done.3, f32[]{:T(128)} %bitcast.47, f32[]{:T(128)} %bitcast.46, f32[]{:T(128)} %bitcast.45, f32[]{:T(128)} %bitcast.44, ...), kind=kLoop, calls=%fused_computation.83 | loop fusion | flops 9953280 | bytes 4243508 | tf_op jit(solution)/shard_map/reduce_sum | solution.py:121
  157.2 4.6 all-to-all-start.2
  162.0 123.4 %while.21 = (s32[]{:T(128)}, f32[16,64,128]{2,1,0:T(8,128)}, bf16[16,64,16,128]{3,2,1,0:T(8,128)(2,1)}, s32[16,64,128]{2,1,0:T(8,128)}, f32[16,512]{1,0:T(8,128)S(1)}, /*index=5*/s32[]{:T(128)}) while((s32[]{:T(128)}, f32[16,64,128]{2,1,0:T(8,128)}, bf16[16,64,16,128]{3,2,1,0:T(8,128)(2,1)}, s32[16,64,128]{2,1,0:T(8,128)}, ...), condition=%wide.region_5.6_spmd, body=%wide.region_3.5_spmd.sunk | while | flops 809885696 | bytes 491609 | solution.py:173
  162.8 6.3 %fusion.105 = f32[64,128]{1,0:T(8,128)S(1)} fusion(s32[64,128]{1,0:T(8,128)S(1)} %dynamic-slice_bitcast_fusion.6, bf16[16,64,16,128]{3,2,1,0:T(8,128)(2,1)} %get-tuple-element.208, s32[]{:T(128)S(6)} %copy.103, f32[16,512]{1,0:T(8,128)S(1)} %get-tuple-element.210), kind=kOutput, calls=%fused_computation.6.clone.1 | convolution fusion | flops 809885696 | bytes 360452 | tf_op jit(solution)/shard_map/while/body/eval_jaxpr/ac,cgp->gap/dot_general | solution.py:170
  170.5 6.3 %fusion.105 = f32[64,128]{1,0:T(8,128)S(1)} fusion(s32[64,128]{1,0:T(8,128)S(1)} %dynamic-slice_bitcast_fusion.6, bf16[16,64,16,128]{3,2,1,0:T(8,128)(2,1)} %get-tuple-element.208, s32[]{:T(128)S(6)} %copy.103, f32[16,512]{1,0:T(8,128)S(1)} %get-tuple-element.210), kind=kOutput, calls=%fused_computation.6.clone.1 | convolution fusion | flops 809885696 | bytes 360452 | tf_op jit(solution)/shard_map/while/body/eval_jaxpr/ac,cgp->gap/dot_general | solution.py:170
  178.2 6.3 %fusion.105 = f32[64,128]{1,0:T(8,128)S(1)} fusion(s32[64,128]{1,0:T(8,128)S(1)} %dynamic-slice_bitcast_fusion.6, bf16[16,64,16,128]{3,2,1,0:T(8,128)(2,1)} %get-tuple-element.208, s32[]{:T(128)S(6)} %copy.103, f32[16,512]{1,0:T(8,128)S(1)} %get-tuple-element.210), kind=kOutput, calls=%fused_computation.6.clone.1 | convolution fusion | flops 809885696 | bytes 360452 | tf_op jit(solution)/shard_map/while/body/eval_jaxpr/ac,cgp->gap/dot_general | solution.py:170
  185.9 6.3 %fusion.105 = f32[64,128]{1,0:T(8,128)S(1)} fusion(s32[64,128]{1,0:T(8,128)S(1)} %dynamic-slice_bitcast_fusion.6, bf16[16,64,16,128]{3,2,1,0:T(8,128)(2,1)} %get-tuple-element.208, s32[]{:T(128)S(6)} %copy.103, f32[16,512]{1,0:T(8,128)S(1)} %get-tuple-element.210), kind=kOutput, calls=%fused_computation.6.clone.1 | convolution fusion | flops 809885696 | bytes 360452 | tf_op jit(solution)/shard_map/while/body/eval_jaxpr/ac,cgp->gap/dot_general | solution.py:170
  193.7 6.3 %fusion.105 = f32[64,128]{1,0:T(8,128)S(1)} fusion(s32[64,128]{1,0:T(8,128)S(1)} %dynamic-slice_bitcast_fusion.6, bf16[16,64,16,128]{3,2,1,0:T(8,128)(2,1)} %get-tuple-element.208, s32[]{:T(128)S(6)} %copy.103, f32[16,512]{1,0:T(8,128)S(1)} %get-tuple-element.210), kind=kOutput, calls=%fused_computation.6.clone.1 | convolution fusion | flops 809885696 | bytes 360452 | tf_op jit(solution)/shard_map/while/body/eval_jaxpr/ac,cgp->gap/dot_general | solution.py:170
  201.4 6.3 %fusion.105 = f32[64,128]{1,0:T(8,128)S(1)} fusion(s32[64,128]{1,0:T(8,128)S(1)} %dynamic-slice_bitcast_fusion.6, bf16[16,64,16,128]{3,2,1,0:T(8,128)(2,1)} %get-tuple-element.208, s32[]{:T(128)S(6)} %copy.103, f32[16,512]{1,0:T(8,128)S(1)} %get-tuple-element.210), kind=kOutput, calls=%fused_computation.6.clone.1 | convolution fusion | flops 809885696 | bytes 360452 | tf_op jit(solution)/shard_map/while/body/eval_jaxpr/ac,cgp->gap/dot_general | solution.py:170
  209.1 6.3 %fusion.105 = f32[64,128]{1,0:T(8,128)S(1)} fusion(s32[64,128]{1,0:T(8,128)S(1)} %dynamic-slice_bitcast_fusion.6, bf16[16,64,16,128]{3,2,1,0:T(8,128)(2,1)} %get-tuple-element.208, s32[]{:T(128)S(6)} %copy.103, f32[16,512]{1,0:T(8,128)S(1)} %get-tuple-element.210), kind=kOutput, calls=%fused_computation.6.clone.1 | convolution fusion | flops 809885696 | bytes 360452 | tf_op jit(solution)/shard_map/while/body/eval_jaxpr/ac,cgp->gap/dot_general | solution.py:170
  216.8 6.3 %fusion.105 = f32[64,128]{1,0:T(8,128)S(1)} fusion(s32[64,128]{1,0:T(8,128)S(1)} %dynamic-slice_bitcast_fusion.6, bf16[16,64,16,128]{3,2,1,0:T(8,128)(2,1)} %get-tuple-element.208, s32[]{:T(128)S(6)} %copy.103, f32[16,512]{1,0:T(8,128)S(1)} %get-tuple-element.210), kind=kOutput, calls=%fused_computation.6.clone.1 | convolution fusion | flops 809885696 | bytes 360452 | tf_op jit(solution)/shard_map/while/body/eval_jaxpr/ac,cgp->gap/dot_general | solution.py:170
  224.5 6.3 %fusion.105 = f32[64,128]{1,0:T(8,128)S(1)} fusion(s32[64,128]{1,0:T(8,128)S(1)} %dynamic-slice_bitcast_fusion.6, bf16[16,64,16,128]{3,2,1,0:T(8,128)(2,1)} %get-tuple-element.208, s32[]{:T(128)S(6)} %copy.103, f32[16,512]{1,0:T(8,128)S(1)} %get-tuple-element.210), kind=kOutput, calls=%fused_computation.6.clone.1 | convolution fusion | flops 809885696 | bytes 360452 | tf_op jit(solution)/shard_map/while/body/eval_jaxpr/ac,cgp->gap/dot_general | solution.py:170
  232.2 6.3 %fusion.105 = f32[64,128]{1,0:T(8,128)S(1)} fusion(s32[64,128]{1,0:T(8,128)S(1)} %dynamic-slice_bitcast_fusion.6, bf16[16,64,16,128]{3,2,1,0:T(8,128)(2,1)} %get-tuple-element.208, s32[]{:T(128)S(6)} %copy.103, f32[16,512]{1,0:T(8,128)S(1)} %get-tuple-element.210), kind=kOutput, calls=%fused_computation.6.clone.1 | convolution fusion | flops 809885696 | bytes 360452 | tf_op jit(solution)/shard_map/while/body/eval_jaxpr/ac,cgp->gap/dot_general | solution.py:170
  239.9 6.3 %fusion.105 = f32[64,128]{1,0:T(8,128)S(1)} fusion(s32[64,128]{1,0:T(8,128)S(1)} %dynamic-slice_bitcast_fusion.6, bf16[16,64,16,128]{3,2,1,0:T(8,128)(2,1)} %get-tuple-element.208, s32[]{:T(128)S(6)} %copy.103, f32[16,512]{1,0:T(8,128)S(1)} %get-tuple-element.210), kind=kOutput, calls=%fused_computation.6.clone.1 | convolution fusion | flops 809885696 | bytes 360452 | tf_op jit(solution)/shard_map/while/body/eval_jaxpr/ac,cgp->gap/dot_general | solution.py:170
  247.7 6.3 %fusion.105 = f32[64,128]{1,0:T(8,128)S(1)} fusion(s32[64,128]{1,0:T(8,128)S(1)} %dynamic-slice_bitcast_fusion.6, bf16[16,64,16,128]{3,2,1,0:T(8,128)(2,1)} %get-tuple-element.208, s32[]{:T(128)S(6)} %copy.103, f32[16,512]{1,0:T(8,128)S(1)} %get-tuple-element.210), kind=kOutput, calls=%fused_computation.6.clone.1 | convolution fusion | flops 809885696 | bytes 360452 | tf_op jit(solution)/shard_map/while/body/eval_jaxpr/ac,cgp->gap/dot_general | solution.py:170
  255.4 6.3 %fusion.105 = f32[64,128]{1,0:T(8,128)S(1)} fusion(s32[64,128]{1,0:T(8,128)S(1)} %dynamic-slice_bitcast_fusion.6, bf16[16,64,16,128]{3,2,1,0:T(8,128)(2,1)} %get-tuple-element.208, s32[]{:T(128)S(6)} %copy.103, f32[16,512]{1,0:T(8,128)S(1)} %get-tuple-element.210), kind=kOutput, calls=%fused_computation.6.clone.1 | convolution fusion | flops 809885696 | bytes 360452 | tf_op jit(solution)/shard_map/while/body/eval_jaxpr/ac,cgp->gap/dot_general | solution.py:170
  263.1 6.3 %fusion.105 = f32[64,128]{1,0:T(8,128)S(1)} fusion(s32[64,128]{1,0:T(8,128)S(1)} %dynamic-slice_bitcast_fusion.6, bf16[16,64,16,128]{3,2,1,0:T(8,128)(2,1)} %get-tuple-element.208, s32[]{:T(128)S(6)} %copy.103, f32[16,512]{1,0:T(8,128)S(1)} %get-tuple-element.210), kind=kOutput, calls=%fused_computation.6.clone.1 | convolution fusion | flops 809885696 | bytes 360452 | tf_op jit(solution)/shard_map/while/body/eval_jaxpr/ac,cgp->gap/dot_general | solution.py:170
  270.8 6.3 %fusion.105 = f32[64,128]{1,0:T(8,128)S(1)} fusion(s32[64,128]{1,0:T(8,128)S(1)} %dynamic-slice_bitcast_fusion.6, bf16[16,64,16,128]{3,2,1,0:T(8,128)(2,1)} %get-tuple-element.208, s32[]{:T(128)S(6)} %copy.103, f32[16,512]{1,0:T(8,128)S(1)} %get-tuple-element.210), kind=kOutput, calls=%fused_computation.6.clone.1 | convolution fusion | flops 809885696 | bytes 360452 | tf_op jit(solution)/shard_map/while/body/eval_jaxpr/ac,cgp->gap/dot_general | solution.py:170
  278.5 6.3 %fusion.105 = f32[64,128]{1,0:T(8,128)S(1)} fusion(s32[64,128]{1,0:T(8,128)S(1)} %dynamic-slice_bitcast_fusion.6, bf16[16,64,16,128]{3,2,1,0:T(8,128)(2,1)} %get-tuple-element.208, s32[]{:T(128)S(6)} %copy.103, f32[16,512]{1,0:T(8,128)S(1)} %get-tuple-element.210), kind=kOutput, calls=%fused_computation.6.clone.1 | convolution fusion | flops 809885696 | bytes 360452 | tf_op jit(solution)/shard_map/while/body/eval_jaxpr/ac,cgp->gap/dot_general | solution.py:170
  285.5 5.8 %all-to-all-start.1 = ((s32[8,128,1]{1,2,0:T(1,128)}), s32[8,128,1]{1,2,0:T(1,128)S(1)}, u32[]{:S(2)}, u32[]{:S(2)}) async-start(s32[8,128,1]{1,2,0:T(1,128)} %slice_bitcast_fusion.1), calls=%async_computation.1 | async-start | bytes 8192 | tf_op jit(solution)/shard_map/all_to_all | solution.py:160
  291.3 1.5 fusion.95
  292.8 4.9 all-to-all-done.1
  297.7 22.3 %all-reduce.2.cloned.1.call-done = f32[1024,128]{1,0:T(8,128)} async-done(((f32[1024,128]{1,0:T(8,128)}), f32[1024,128]{1,0:T(8,128)}) %all-reduce.2.cloned.1.call-update) | async-done | bytes 524304 | tf_op jit(solution)/shard_map/psum | solution.py:176
  321.4 147.6 %while.22 = (s32[]{:T(128)}, f32[16,512]{1,0:T(8,128)S(1)}, bf16[16,64,16,128]{3,2,1,0:T(8,128)(2,1)}, f32[16,64,128]{2,1,0:T(8,128)S(1)}, s32[16,64,128]{2,1,0:T(8,128)}, /*index=5*/s32[]{:T(128)}, s32[]{:T(128)}) while((s32[]{:T(128)}, f32[16,512]{1,0:T(8,128)S(1)}, bf16[16,64,16,128]{3,2,1,0:T(8,128)(2,1)}, ...), condition=%wide.region_8.9_spmd.clone, body=%wide.region_7.8_spmd.clone.sunk | while | flops 809779200 | bytes 524395 | solution.py:189
  322.2 8.4 %fusion.106 = f32[16,512]{1,0:T(8,128)S(1)} fusion(s32[64,128]{1,0:T(8,128)S(1)} %dynamic-slice_bitcast_fusion.7, f32[64,128]{1,0:T(8,128)S(1)} %dynamic-slice_bitcast_fusion.8, bf16[16,64,16,128]{3,2,1,0:T(8,128)(2,1)} %get-tuple-element.228, s32[]{:T(128)S(6)} %copy.110, f32[16,512]{1,0:T(8,128)S(1)} %get-tuple-element.220, pred[]{:T(512)S(6)} %compare.3), kind=kOutput, calls=%fused_computation.14.clone.1 | convolution fusion | flops 809779200 | bytes 393221 | tf_op jit(solution)/shard_map/while/body/eval_jaxpr/gap,cgp->ac/dot_general | solution.py:185
  331.4 8.4 %fusion.106 = f32[16,512]{1,0:T(8,128)S(1)} fusion(s32[64,128]{1,0:T(8,128)S(1)} %dynamic-slice_bitcast_fusion.7, f32[64,128]{1,0:T(8,128)S(1)} %dynamic-slice_bitcast_fusion.8, bf16[16,64,16,128]{3,2,1,0:T(8,128)(2,1)} %get-tuple-element.228, s32[]{:T(128)S(6)} %copy.110, f32[16,512]{1,0:T(8,128)S(1)} %get-tuple-element.220, pred[]{:T(512)S(6)} %compare.3), kind=kOutput, calls=%fused_computation.14.clone.1 | convolution fusion | flops 809779200 | bytes 393221 | tf_op jit(solution)/shard_map/while/body/eval_jaxpr/gap,cgp->ac/dot_general | solution.py:185
  340.7 8.4 %fusion.106 = f32[16,512]{1,0:T(8,128)S(1)} fusion(s32[64,128]{1,0:T(8,128)S(1)} %dynamic-slice_bitcast_fusion.7, f32[64,128]{1,0:T(8,128)S(1)} %dynamic-slice_bitcast_fusion.8, bf16[16,64,16,128]{3,2,1,0:T(8,128)(2,1)} %get-tuple-element.228, s32[]{:T(128)S(6)} %copy.110, f32[16,512]{1,0:T(8,128)S(1)} %get-tuple-element.220, pred[]{:T(512)S(6)} %compare.3), kind=kOutput, calls=%fused_computation.14.clone.1 | convolution fusion | flops 809779200 | bytes 393221 | tf_op jit(solution)/shard_map/while/body/eval_jaxpr/gap,cgp->ac/dot_general | solution.py:185
  349.9 8.4 %fusion.106 = f32[16,512]{1,0:T(8,128)S(1)} fusion(s32[64,128]{1,0:T(8,128)S(1)} %dynamic-slice_bitcast_fusion.7, f32[64,128]{1,0:T(8,128)S(1)} %dynamic-slice_bitcast_fusion.8, bf16[16,64,16,128]{3,2,1,0:T(8,128)(2,1)} %get-tuple-element.228, s32[]{:T(128)S(6)} %copy.110, f32[16,512]{1,0:T(8,128)S(1)} %get-tuple-element.220, pred[]{:T(512)S(6)} %compare.3), kind=kOutput, calls=%fused_computation.14.clone.1 | convolution fusion | flops 809779200 | bytes 393221 | tf_op jit(solution)/shard_map/while/body/eval_jaxpr/gap,cgp->ac/dot_general | solution.py:185
  359.1 8.4 %fusion.106 = f32[16,512]{1,0:T(8,128)S(1)} fusion(s32[64,128]{1,0:T(8,128)S(1)} %dynamic-slice_bitcast_fusion.7, f32[64,128]{1,0:T(8,128)S(1)} %dynamic-slice_bitcast_fusion.8, bf16[16,64,16,128]{3,2,1,0:T(8,128)(2,1)} %get-tuple-element.228, s32[]{:T(128)S(6)} %copy.110, f32[16,512]{1,0:T(8,128)S(1)} %get-tuple-element.220, pred[]{:T(512)S(6)} %compare.3), kind=kOutput, calls=%fused_computation.14.clone.1 | convolution fusion | flops 809779200 | bytes 393221 | tf_op jit(solution)/shard_map/while/body/eval_jaxpr/gap,cgp->ac/dot_general | solution.py:185
  368.3 8.4 %fusion.106 = f32[16,512]{1,0:T(8,128)S(1)} fusion(s32[64,128]{1,0:T(8,128)S(1)} %dynamic-slice_bitcast_fusion.7, f32[64,128]{1,0:T(8,128)S(1)} %dynamic-slice_bitcast_fusion.8, bf16[16,64,16,128]{3,2,1,0:T(8,128)(2,1)} %get-tuple-element.228, s32[]{:T(128)S(6)} %copy.110, f32[16,512]{1,0:T(8,128)S(1)} %get-tuple-element.220, pred[]{:T(512)S(6)} %compare.3), kind=kOutput, calls=%fused_computation.14.clone.1 | convolution fusion | flops 809779200 | bytes 393221 | tf_op jit(solution)/shard_map/while/body/eval_jaxpr/gap,cgp->ac/dot_general | solution.py:185
  377.6 8.4 %fusion.106 = f32[16,512]{1,0:T(8,128)S(1)} fusion(s32[64,128]{1,0:T(8,128)S(1)} %dynamic-slice_bitcast_fusion.7, f32[64,128]{1,0:T(8,128)S(1)} %dynamic-slice_bitcast_fusion.8, bf16[16,64,16,128]{3,2,1,0:T(8,128)(2,1)} %get-tuple-element.228, s32[]{:T(128)S(6)} %copy.110, f32[16,512]{1,0:T(8,128)S(1)} %get-tuple-element.220, pred[]{:T(512)S(6)} %compare.3), kind=kOutput, calls=%fused_computation.14.clone.1 | convolution fusion | flops 809779200 | bytes 393221 | tf_op jit(solution)/shard_map/while/body/eval_jaxpr/gap,cgp->ac/dot_general | solution.py:185
  386.8 8.4 %fusion.106 = f32[16,512]{1,0:T(8,128)S(1)} fusion(s32[64,128]{1,0:T(8,128)S(1)} %dynamic-slice_bitcast_fusion.7, f32[64,128]{1,0:T(8,128)S(1)} %dynamic-slice_bitcast_fusion.8, bf16[16,64,16,128]{3,2,1,0:T(8,128)(2,1)} %get-tuple-element.228, s32[]{:T(128)S(6)} %copy.110, f32[16,512]{1,0:T(8,128)S(1)} %get-tuple-element.220, pred[]{:T(512)S(6)} %compare.3), kind=kOutput, calls=%fused_computation.14.clone.1 | convolution fusion | flops 809779200 | bytes 393221 | tf_op jit(solution)/shard_map/while/body/eval_jaxpr/gap,cgp->ac/dot_general | solution.py:185
  396.0 8.4 %fusion.106 = f32[16,512]{1,0:T(8,128)S(1)} fusion(s32[64,128]{1,0:T(8,128)S(1)} %dynamic-slice_bitcast_fusion.7, f32[64,128]{1,0:T(8,128)S(1)} %dynamic-slice_bitcast_fusion.8, bf16[16,64,16,128]{3,2,1,0:T(8,128)(2,1)} %get-tuple-element.228, s32[]{:T(128)S(6)} %copy.110, f32[16,512]{1,0:T(8,128)S(1)} %get-tuple-element.220, pred[]{:T(512)S(6)} %compare.3), kind=kOutput, calls=%fused_computation.14.clone.1 | convolution fusion | flops 809779200 | bytes 393221 | tf_op jit(solution)/shard_map/while/body/eval_jaxpr/gap,cgp->ac/dot_general | solution.py:185
  405.2 8.4 %fusion.106 = f32[16,512]{1,0:T(8,128)S(1)} fusion(s32[64,128]{1,0:T(8,128)S(1)} %dynamic-slice_bitcast_fusion.7, f32[64,128]{1,0:T(8,128)S(1)} %dynamic-slice_bitcast_fusion.8, bf16[16,64,16,128]{3,2,1,0:T(8,128)(2,1)} %get-tuple-element.228, s32[]{:T(128)S(6)} %copy.110, f32[16,512]{1,0:T(8,128)S(1)} %get-tuple-element.220, pred[]{:T(512)S(6)} %compare.3), kind=kOutput, calls=%fused_computation.14.clone.1 | convolution fusion | flops 809779200 | bytes 393221 | tf_op jit(solution)/shard_map/while/body/eval_jaxpr/gap,cgp->ac/dot_general | solution.py:185
  414.5 8.4 %fusion.106 = f32[16,512]{1,0:T(8,128)S(1)} fusion(s32[64,128]{1,0:T(8,128)S(1)} %dynamic-slice_bitcast_fusion.7, f32[64,128]{1,0:T(8,128)S(1)} %dynamic-slice_bitcast_fusion.8, bf16[16,64,16,128]{3,2,1,0:T(8,128)(2,1)} %get-tuple-element.228, s32[]{:T(128)S(6)} %copy.110, f32[16,512]{1,0:T(8,128)S(1)} %get-tuple-element.220, pred[]{:T(512)S(6)} %compare.3), kind=kOutput, calls=%fused_computation.14.clone.1 | convolution fusion | flops 809779200 | bytes 393221 | tf_op jit(solution)/shard_map/while/body/eval_jaxpr/gap,cgp->ac/dot_general | solution.py:185
  423.7 8.4 %fusion.106 = f32[16,512]{1,0:T(8,128)S(1)} fusion(s32[64,128]{1,0:T(8,128)S(1)} %dynamic-slice_bitcast_fusion.7, f32[64,128]{1,0:T(8,128)S(1)} %dynamic-slice_bitcast_fusion.8, bf16[16,64,16,128]{3,2,1,0:T(8,128)(2,1)} %get-tuple-element.228, s32[]{:T(128)S(6)} %copy.110, f32[16,512]{1,0:T(8,128)S(1)} %get-tuple-element.220, pred[]{:T(512)S(6)} %compare.3), kind=kOutput, calls=%fused_computation.14.clone.1 | convolution fusion | flops 809779200 | bytes 393221 | tf_op jit(solution)/shard_map/while/body/eval_jaxpr/gap,cgp->ac/dot_general | solution.py:185
  432.9 8.4 %fusion.106 = f32[16,512]{1,0:T(8,128)S(1)} fusion(s32[64,128]{1,0:T(8,128)S(1)} %dynamic-slice_bitcast_fusion.7, f32[64,128]{1,0:T(8,128)S(1)} %dynamic-slice_bitcast_fusion.8, bf16[16,64,16,128]{3,2,1,0:T(8,128)(2,1)} %get-tuple-element.228, s32[]{:T(128)S(6)} %copy.110, f32[16,512]{1,0:T(8,128)S(1)} %get-tuple-element.220, pred[]{:T(512)S(6)} %compare.3), kind=kOutput, calls=%fused_computation.14.clone.1 | convolution fusion | flops 809779200 | bytes 393221 | tf_op jit(solution)/shard_map/while/body/eval_jaxpr/gap,cgp->ac/dot_general | solution.py:185
  442.1 8.4 %fusion.106 = f32[16,512]{1,0:T(8,128)S(1)} fusion(s32[64,128]{1,0:T(8,128)S(1)} %dynamic-slice_bitcast_fusion.7, f32[64,128]{1,0:T(8,128)S(1)} %dynamic-slice_bitcast_fusion.8, bf16[16,64,16,128]{3,2,1,0:T(8,128)(2,1)} %get-tuple-element.228, s32[]{:T(128)S(6)} %copy.110, f32[16,512]{1,0:T(8,128)S(1)} %get-tuple-element.220, pred[]{:T(512)S(6)} %compare.3), kind=kOutput, calls=%fused_computation.14.clone.1 | convolution fusion | flops 809779200 | bytes 393221 | tf_op jit(solution)/shard_map/while/body/eval_jaxpr/gap,cgp->ac/dot_general | solution.py:185
  451.4 8.4 %fusion.106 = f32[16,512]{1,0:T(8,128)S(1)} fusion(s32[64,128]{1,0:T(8,128)S(1)} %dynamic-slice_bitcast_fusion.7, f32[64,128]{1,0:T(8,128)S(1)} %dynamic-slice_bitcast_fusion.8, bf16[16,64,16,128]{3,2,1,0:T(8,128)(2,1)} %get-tuple-element.228, s32[]{:T(128)S(6)} %copy.110, f32[16,512]{1,0:T(8,128)S(1)} %get-tuple-element.220, pred[]{:T(512)S(6)} %compare.3), kind=kOutput, calls=%fused_computation.14.clone.1 | convolution fusion | flops 809779200 | bytes 393221 | tf_op jit(solution)/shard_map/while/body/eval_jaxpr/gap,cgp->ac/dot_general | solution.py:185
  460.6 8.4 %fusion.106 = f32[16,512]{1,0:T(8,128)S(1)} fusion(s32[64,128]{1,0:T(8,128)S(1)} %dynamic-slice_bitcast_fusion.7, f32[64,128]{1,0:T(8,128)S(1)} %dynamic-slice_bitcast_fusion.8, bf16[16,64,16,128]{3,2,1,0:T(8,128)(2,1)} %get-tuple-element.228, s32[]{:T(128)S(6)} %copy.110, f32[16,512]{1,0:T(8,128)S(1)} %get-tuple-element.220, pred[]{:T(512)S(6)} %compare.3), kind=kOutput, calls=%fused_computation.14.clone.1 | convolution fusion | flops 809779200 | bytes 393221 | tf_op jit(solution)/shard_map/while/body/eval_jaxpr/gap,cgp->ac/dot_general | solution.py:185
  471.3 5.3 collective-permute-start.9
  477.1 1.9 collective-permute-done.10
  479.1 5.7 %collective-permute-done.9 = f32[16,32,4]{2,0,1:T(8,128)} collective-permute-done((f32[16,32,4]{2,0,1:T(8,128)S(1)}, f32[16,32,4]{2,0,1:T(8,128)}, u32[]{:S(2)}, u32[]{:S(2)}) %collective-permute-start.9) | collective-permute-done | bytes 8224 | tf_op jit(solution)/shard_map/ppermute | solution.py:41
  484.7 10.3 %fusion.25 = bf16[16,32,512]{2,0,1:T(8,128)(2,1)} fusion(f32[16,32,512]{2,0,1:T(8,128)S(1)} %fusion.71, f32[16,32,4]{2,0,1:T(8,128)} %collective-permute-done.10, f32[16,32,4]{2,0,1:T(8,128)} %collective-permute-done.9, f32[16,1,32,512]{3,0,2,1:T(8,128)S(1)} %get-tuple-element.100, f32[]{:T(128)S(6)} %mul.235, f32[16,512]{1,0:T(8,128)S(1)} %get-tuple-element.60, ...), kind=kLoop, calls=%fused_computation.61 | loop fusion | flops 7077888 | bytes 2670628 | tf_op jit(solution)/shard_map/convert_element_type | solution.py:195
  495.1 23.0 %all-gather.5.cloned.1.call-done = bf16[64,32,512]{2,0,1:T(8,128)(2,1)} async-done(((bf16[16,32,512]{2,0,1:T(8,128)(2,1)}), bf16[64,32,512]{2,0,1:T(8,128)(2,1)}) %all-gather.5.cloned.1.call-update) | async-done | bytes 2097168 | tf_op jit(solution)/shard_map/all_gather | solution.py:200
  518.0 2.5 convolution_add_fusion
  520.5 1.6 copy.63
  (143 shorter events, 70.4 us)
Async XLA Ops:
  15.6 7.5 %copy-start = (f32[16,32,512]{2,1,0:T(8,128)S(1)}, f32[16,32,512]{2,1,0:T(8,128)}, u32[]{:S(2)}) copy-start(f32[16,32,512]{2,1,0:T(8,128)} %param.13) | copy-start | bytes 3145732
  15.6 141.5 %all-to-all-start = ((bf16[1024,16,128]{2,1,0:T(8,128)(2,1)}), bf16[1024,16,128]{2,1,0:T(8,128)(2,1)}, u32[]{:S(2)}, u32[]{:S(2)}) async-start(bf16[1024,16,128]{2,1,0:T(8,128)(2,1)} %bitcast.133), calls=%async_computation | async-start | bytes 8388608 | tf_op jit(solution)/shard_map/all_to_all | solution.py:155
  23.0 1.5 copy-start.7
  23.0 1.7 copy-start.8
  23.1 105.8 %all-gather.3.cloned.1.call-start = ((), (), s32[]{:S(2)}) async-start(), calls=%async_computation.3 | async-start | bytes 2621440 | tf_op jit(solution)/shard_map/all_gather | solution.py:114
  26.1 0.8 copy-start.2
  28.2 30.8 %collective-permute-start = (s32[128,128]{1,0:T(8,128)}, s32[128,128]{1,0:T(8,128)}, u32[]{:S(2)}, u32[]{:S(2)}) collective-permute-start(s32[128,128]{1,0:T(8,128)} %bitcast.23), channel_id=1, source_target_pairs={{0,4},{4,0},{8,12},{12,8},{16,20},{20,16},{24,28},{28,24},{1,5},{5... | collective-permute-start | bytes 196616 | tf_op jit(solution)/shard_map/ppermute | solution.py:29
  30.9 63.5 %collective-permute-start.1 = (s32[128,128]{1,0:T(8,128)}, s32[128,128]{1,0:T(8,128)}, u32[]{:S(2)}, u32[]{:S(2)}) collective-permute-start(s32[128,128]{1,0:T(8,128)} %bitcast.25), channel_id=1, source_target_pairs={{0,8},{4,12},{8,0},{12,4},{16,24},{20,28},{24,16},{28,20},{1,9},{5... | collective-permute-start | bytes 196616 | tf_op jit(solution)/shard_map/ppermute | solution.py:29
  33.1 66.5 %collective-permute-start.2 = (s32[128,128]{1,0:T(8,128)}, s32[128,128]{1,0:T(8,128)}, u32[]{:S(2)}, u32[]{:S(2)}) collective-permute-start(s32[128,128]{1,0:T(8,128)} %bitcast.27), channel_id=1, source_target_pairs={{0,12},{4,8},{8,4},{12,0},{16,28},{20,24},{24,20},{28,16},{1,13},{... | collective-permute-start | bytes 196616 | tf_op jit(solution)/shard_map/ppermute | solution.py:29
  33.8 90.9 %collective-permute-start.3 = (s32[128,128]{1,0:T(8,128)}, s32[128,128]{1,0:T(8,128)}, u32[]{:S(2)}, u32[]{:S(2)}) collective-permute-start(s32[128,128]{1,0:T(8,128)} %bitcast.29), channel_id=1, source_target_pairs={{0,16},{4,20},{8,24},{12,28},{16,0},{20,4},{24,8},{28,12},{1,17},{... | collective-permute-start | bytes 196616 | tf_op jit(solution)/shard_map/ppermute | solution.py:29
  36.8 10.5 %copy-start.6 = (f32[4]{0:T(128)S(1)}, f32[4]{0:T(128)}, u32[]{:S(2)}) copy-start(f32[4]{0:T(128)} %param.15) | copy-start | bytes 52
  37.5 89.3 %collective-permute-start.4 = (s32[128,128]{1,0:T(8,128)}, s32[128,128]{1,0:T(8,128)}, u32[]{:S(2)}, u32[]{:S(2)}) collective-permute-start(s32[128,128]{1,0:T(8,128)} %bitcast.31), channel_id=1, source_target_pairs={{0,20},{4,16},{8,28},{12,24},{16,4},{20,0},{24,12},{28,8},{1,21},{... | collective-permute-start | bytes 196616 | tf_op jit(solution)/shard_map/ppermute | solution.py:29
  38.9 11.7 %copy-start.1 = (bf16[16,4,32,512]{3,2,1,0:T(8,128)(2,1)S(1)}, bf16[16,4,32,512]{3,2,1,0:T(8,128)(2,1)}, u32[]{:S(2)}) copy-start(bf16[16,4,32,512]{3,2,1,0:T(8,128)(2,1)} %param.14) | copy-start | bytes 6291460
  50.6 8.3 %copy-start.5 = (s32[1,128,128]{2,1,0:T(8,128)S(1)}, s32[1,128,128]{2,1,0:T(8,128)}, u32[]{:S(2)}) copy-start(s32[1,128,128]{2,1,0:T(8,128)} %copy.58) | copy-start | bytes 196612
  50.6 43.7 %copy-start.4 = (s32[1,128,128]{2,1,0:T(8,128)S(1)}, s32[1,128,128]{2,1,0:T(8,128)}, u32[]{:S(2)}) copy-start(s32[1,128,128]{2,1,0:T(8,128)} %copy.59) | copy-start | bytes 196612
  59.0 69.2 %collective-permute-start.5 = (s32[128,128]{1,0:T(8,128)S(1)}, s32[128,128]{1,0:T(8,128)S(1)}, u32[]{:S(2)}, u32[]{:S(2)}) collective-permute-start(s32[128,128]{1,0:T(8,128)S(1)} %bitcast.144), channel_id=1, source_target_pairs={{0,24},{4,28},{8,16},{12,20},{16,8},{20,12},{24,0},{28,4},{1,25},{... | collective-permute-start | bytes 196616 | tf_op jit(solution)/shard_map/ppermute | solution.py:29
  94.4 42.5 %collective-permute-start.6 = (s32[128,128]{1,0:T(8,128)S(1)}, s32[128,128]{1,0:T(8,128)S(1)}, u32[]{:S(2)}, u32[]{:S(2)}) collective-permute-start(s32[128,128]{1,0:T(8,128)S(1)} %bitcast.143), channel_id=1, source_target_pairs={{0,28},{4,24},{8,20},{12,16},{16,12},{20,8},{24,4},{28,0},{1,29},{... | collective-permute-start | bytes 196616 | tf_op jit(solution)/shard_map/ppermute | solution.py:29
  131.0 9.0 %collective-permute-start.8 = (f32[16,32,4]{2,0,1:T(8,128)S(1)}, f32[16,32,4]{2,0,1:T(8,128)S(1)}, u32[]{:S(2)}, u32[]{:S(2)}) collective-permute-start(f32[16,32,4]{2,0,1:T(8,128)S(1)} %get-tuple-element.108), channel_id=1, source_target_pairs={{4,0},{8,4},{12,8},{16,12},{20,16},{24,20},{28,24},{5,1},{9,5},{13... | collective-permute-start | bytes 24584 | tf_op jit(solution)/shard_map/ppermute | solution.py:42
  132.3 11.5 %collective-permute-start.7 = (f32[16,32,4]{2,0,1:T(8,128)S(1)}, f32[16,32,4]{2,0,1:T(8,128)S(1)}, u32[]{:S(2)}, u32[]{:S(2)}) collective-permute-start(f32[16,32,4]{2,0,1:T(8,128)S(1)} %get-tuple-element.107), channel_id=1, source_target_pairs={{0,4},{4,8},{8,12},{12,16},{16,20},{20,24},{24,28},{1,5},{5,9},{9,... | collective-permute-start | bytes 24584 | tf_op jit(solution)/shard_map/ppermute | solution.py:41
  143.8 0.7 copy-start.3
  157.2 128.3 %all-to-all-start.2 = ((bf16[1024,2,128]{2,1,0:T(2,128)(2,1)}), bf16[1024,2,128]{2,1,0:T(2,128)(2,1)S(1)}, u32[]{:S(2)}, u32[]{:S(2)}) async-start(bf16[1024,2,128]{2,1,0:T(2,128)(2,1)} %copy.50), calls=%async_computation.2 | async-start | bytes 1048576 | tf_op jit(solution)/shard_map/all_to_all | solution.py:156
  161.8 158.2 %all-reduce.2.cloned.1.call-start = ((), (), s32[]{:S(2)}) async-start(), calls=%async_computation.4 | async-start | bytes 1048576 | tf_op jit(solution)/shard_map/psum | solution.py:176
  285.5 12.2 %all-to-all-start.1 = ((s32[8,128,1]{1,2,0:T(1,128)}), s32[8,128,1]{1,2,0:T(1,128)S(1)}, u32[]{:S(2)}, u32[]{:S(2)}) async-start(s32[8,128,1]{1,2,0:T(1,128)} %slice_bitcast_fusion.1), calls=%async_computation.1 | async-start | bytes 8192 | tf_op jit(solution)/shard_map/all_to_all | solution.py:160
  291.3 226.8 %all-gather.5.cloned.1.call-start = ((), (), s32[]{:S(2)}) async-start(), calls=%async_computation.5 | async-start | bytes 2621440 | tf_op jit(solution)/shard_map/all_gather | solution.py:200
  470.0 9.1 %collective-permute-start.10 = (f32[16,32,4]{2,0,1:T(8,128)}, f32[16,32,4]{2,0,1:T(8,128)}, u32[]{:S(2)}, u32[]{:S(2)}) collective-permute-start(f32[16,32,4]{2,0,1:T(8,128)} %get-tuple-element.106), channel_id=1, source_target_pairs={{4,0},{8,4},{12,8},{16,12},{20,16},{24,20},{28,24},{5,1},{9,5},{13... | collective-permute-start | bytes 24584 | tf_op jit(solution)/shard_map/ppermute | solution.py:42
  471.3 13.4 %collective-permute-start.9 = (f32[16,32,4]{2,0,1:T(8,128)S(1)}, f32[16,32,4]{2,0,1:T(8,128)}, u32[]{:S(2)}, u32[]{:S(2)}) collective-permute-start(f32[16,32,4]{2,0,1:T(8,128)S(1)} %get-tuple-element.105), channel_id=1, source_target_pairs={{0,4},{4,8},{8,12},{12,16},{16,20},{20,24},{24,28},{1,5},{5,9},{9,... | collective-permute-start | bytes 24584 | tf_op jit(solution)/shard_map/ppermute | solution.py:41
Sparse Core Ops, SparseCore 0:
  25.5 23.9 all-gather.2
  285.6 34.3 all-reduce.1
  495.2 22.7 all-gather.4
